TPU v7x, 32 devices: a whole 2x2x4 slice. The times are simulated.
32 devices in a mesh: region: 2 (over x), sub: 16 (over z, y, core).
Axes of the slice: x: 2, y: 2, z: 4, core: 2. Of those that a mesh axis runs over, the one named last changes fastest.
Arguments:
- right_side: bfloat16 [2, 16, 1024, 256], P('region', 'sub'), may hold values from -6 to 6
- local_inverse: bfloat16 [2, 16, 1024, 1024], P('region', 'sub')
- coupling: bfloat16 [2, 16, 4, 256, 256], P('region', 'sub'), may hold values from -0.75 to 0.75
- margin_blocks: int32 [4, 2, 16, 2], P(None, 'region', 'sub'), may hold values from 0 to 7, as said below
- partner: int32 [4, 32], replicated, may hold values from 0 to 31, as said below
- restriction: bfloat16 [2, 16, 64, 1024], P('region', 'sub'), may hold values from -0.375 to 0.375
- coarse_rows: bfloat16 [2, 1024, 1024], P('region', 'sub')
Outputs:
- solution: bfloat16 [2, 16, 1024, 256], P('region', 'sub')
Inputs may be any that keep to these rules, and one draw needn't show every extreme that they name: `margin_blocks`: for each colour, subdomain and k, a block number below 8; the 2 numbers of one colour and subdomain are distinct. For each colour a perfect matching of all subdomains: the partner of a subdomain's partner is the subdomain itself, and no subdomain is its own partner.
All inputs are finite; a program needn't handle non-finite values.
Results may differ from a plain program's by a relative error of at most 0.0052.
Values may be sent and summed in bfloat16 or wider, within the bound.
A program may use at most 64 MiB of HBM per device.

v0:
```python
import jax
import jax.numpy as jnp
from jax import lax
from jax.sharding import PartitionSpec as P

BLK = 128
OVL_BLK = 2
COLORS = 4


def shards(right_side, local_inverse, coupling, margin_blocks, partner, restriction, coarse_rows):
    inverse = local_inverse[0, 0]
    tile_set = coupling[0, 0]
    own_blocks = margin_blocks[:, 0, 0, :]
    row_count = inverse.shape[0]
    columns = right_side.shape[-1]
    block_count = row_count // BLK
    span_rows = tile_set.shape[-1]
    sub_peers = lax.axis_size("sub")
    region_peers = lax.axis_size("region")
    all_peers = sub_peers * region_peers
    piece_len = span_rows * columns // all_peers
    residual = right_side[0, 0].astype(jnp.float32)
    accumulated = jnp.zeros(residual.shape, jnp.float32)
    block_ids = jnp.arange(block_count, dtype=jnp.int32)
    for colour in range(COLORS):
        picked = own_blocks[colour]
        tiled = residual.reshape(block_count, BLK, columns)
        sent_rows = jnp.take(tiled, picked, axis=0).reshape(span_rows, columns).astype(jnp.bfloat16)
        pieces = sent_rows.reshape(region_peers, sub_peers, piece_len)
        relayed = lax.all_to_all(
            lax.all_to_all(pieces, "region", split_axis=0, concat_axis=0, tiled=True),
            "sub",
            split_axis=1,
            concat_axis=1,
            tiled=True,
        )
        relayed = jnp.take(relayed.reshape(all_peers, piece_len), partner[colour], axis=0)
        returned = lax.all_to_all(
            lax.all_to_all(
                relayed.reshape(region_peers, sub_peers, piece_len),
                "region",
                split_axis=0,
                concat_axis=0,
                tiled=True,
            ),
            "sub",
            split_axis=1,
            concat_axis=1,
            tiled=True,
        )
        received = returned.reshape(span_rows, columns)
        coupled = jnp.dot(tile_set[colour], received, preferred_element_type=jnp.float32)
        one_hot = (picked[:, None] == block_ids[None, :]).astype(jnp.float32)
        added = jnp.einsum(
            "kb,kin->bin",
            one_hot,
            coupled.reshape(OVL_BLK, BLK, columns),
            precision=lax.Precision.HIGHEST,
        )
        widened = residual + added.reshape(row_count, columns)
        shaped = widened.astype(jnp.bfloat16)
        correction = jnp.dot(inverse, shaped, preferred_element_type=jnp.float32)
        accumulated = accumulated + correction
        residual = widened - 0.25 * correction
    settled = residual.astype(jnp.bfloat16)
    own_restriction = restriction[0, 0]
    projected = jnp.dot(own_restriction, settled, preferred_element_type=jnp.float32).astype(
        jnp.bfloat16
    )
    own_rows = coarse_rows[0]
    coarse = jnp.dot(
        own_rows,
        lax.all_gather(projected, "sub", axis=0, tiled=True),
        preferred_element_type=jnp.float32,
    ).astype(jnp.bfloat16)
    lifted = lax.dot_general(
        own_restriction, coarse, (((0,), (0,)), ((), ())), preferred_element_type=jnp.float32
    )
    return (accumulated + lifted).astype(jnp.bfloat16)[None, None]


def solution(mesh):
    placed = (
        P("region", "sub", None, None),
        P("region", "sub", None, None),
        P("region", "sub", None, None, None),
        P(None, "region", "sub", None),
        P(),
        P("region", "sub", None, None),
        P("region", "sub", None),
    )
    return jax.shard_map(
        shards,
        mesh=mesh,
        in_specs=placed,
        out_specs=P("region", "sub", None, None),
        check_vma=False,
    )
```

profile of v0, /device:TPU:1, one launch (start us, length us, event | category | flops | bytes accessed | tf_op | source)
XLA Modules:
  0.0 221.6 jit_solution(6520349516597795910)
XLA Ops:
  0.0 1.1 slice_reduce_fusion
  1.1 2.0 copy.96
  3.2 1.2 copy.97
  5.2 6.4 %all_to_all.80 = bf16[2,16,2048]{2,1,0:T(8,128)(2,1)S(1)} all-to-all(bf16[2,16,2048]{2,1,0:T(8,128)(2,1)S(1)} %convert_element_type.77), channel_id=1, replica_groups=mesh['region'=2,'sub'=16] {'region'}, dimensions={0} | all-to-all | bytes 262144 | tf_op jit(solution)/shard_map/all_to_all | solution.py:32
  12.4 8.0 %all-to-all-start.1 = ((bf16[2,16,2048]{2,0,1:T(2,128)(2,1)}), bf16[2,16,2048]{2,0,1:T(2,128)(2,1)S(1)}, u32[]{:S(2)}, u32[]{:S(2)}) async-start(bf16[2,16,2048]{2,0,1:T(2,128)(2,1)} %copy.98), calls=%async_computation.1 | async-start | bytes 262144 | tf_op jit(solution)/shard_map/all_to_all | solution.py:31
  20.4 6.8 %all-to-all-done.1 = bf16[2,16,2048]{2,0,1:T(2,128)(2,1)S(1)} async-done(((bf16[2,16,2048]{2,0,1:T(2,128)(2,1)}), bf16[2,16,2048]{2,0,1:T(2,128)(2,1)S(1)}, u32[]{:S(2)}, u32[]{:S(2)}) %all-to-all-start.1) | async-done | bytes 131104 | tf_op jit(solution)/shard_map/all_to_all | solution.py:31
  28.0 5.7 %all_to_all.81 = bf16[2,16,2048]{2,1,0:T(8,128)(2,1)S(1)} all-to-all(bf16[2,16,2048]{2,1,0:T(8,128)(2,1)S(1)} %bitcast.172), channel_id=1, replica_groups=mesh['region'=2,'sub'=16] {'region'}, dimensions={0} | all-to-all | bytes 262144 | tf_op jit(solution)/shard_map/all_to_all | solution.py:40
  34.5 5.6 %all-to-all-start.3 = ((bf16[2,16,2048]{2,0,1:T(2,128)(2,1)}), bf16[2,16,2048]{2,0,1:T(2,128)(2,1)S(1)}, u32[]{:S(2)}, u32[]{:S(2)}) async-start(bf16[2,16,2048]{2,0,1:T(2,128)(2,1)} %copy.100), calls=%async_computation.3 | async-start | bytes 262144 | tf_op jit(solution)/shard_map/all_to_all | solution.py:39
  40.1 6.9 %all-to-all-done.3 = bf16[2,16,2048]{2,0,1:T(2,128)(2,1)S(1)} async-done(((bf16[2,16,2048]{2,0,1:T(2,128)(2,1)}), bf16[2,16,2048]{2,0,1:T(2,128)(2,1)S(1)}, u32[]{:S(2)}, u32[]{:S(2)}) %all-to-all-start.3) | async-done | bytes 131104 | tf_op jit(solution)/shard_map/all_to_all | solution.py:39
  47.2 1.1 fusion.30
  48.3 1.3 fusion.12
  49.6 0.9 copy.104
  50.9 1.3 copy.106
  52.2 3.3 %bitcast_subtract_fusion.3 = (f32[1024,256]{0,1:T(8,128)S(1)}, f32[256,1024]{1,0:T(8,128)}) fusion(f32[1024,256]{0,1:T(8,128)} %copy.106, bf16[1,1,1024,256]{2,3,1,0:T(8,128)(2,1)} %copy.96, bf16[1024,256]{1,0:T(8,128)(2,1)} %bitcast.164, bf16[1,1,1024,1024]{3,2,1,0:T(8,128)(2,1)S(1)} %copy-done), kind=kOutput, calls=%fused_computation.29 | convolution fusion | flops 537919488 | bytes 6291456 | tf_op jit(solution)/shard_map/dot_general | solution.py:63
  55.5 1.0 copy.135
  56.5 1.6 gather_fusion.2
  58.3 5.7 %all_to_all.82 = bf16[2,16,2048]{2,1,0:T(8,128)(2,1)S(1)} all-to-all(bf16[2,16,2048]{2,1,0:T(8,128)(2,1)S(1)} %convert_element_type.83), channel_id=1, replica_groups=mesh['region'=2,'sub'=16] {'region'}, dimensions={0} | all-to-all | bytes 262144 | tf_op jit(solution)/shard_map/all_to_all | solution.py:32
  64.8 5.6 %all-to-all-start.5 = ((bf16[2,16,2048]{2,0,1:T(2,128)(2,1)}), bf16[2,16,2048]{2,0,1:T(2,128)(2,1)S(1)}, u32[]{:S(2)}, u32[]{:S(2)}) async-start(bf16[2,16,2048]{2,0,1:T(2,128)(2,1)} %copy.108), calls=%async_computation.5 | async-start | bytes 262144 | tf_op jit(solution)/shard_map/all_to_all | solution.py:31
  70.4 6.9 %all-to-all-done.5 = bf16[2,16,2048]{2,0,1:T(2,128)(2,1)S(1)} async-done(((bf16[2,16,2048]{2,0,1:T(2,128)(2,1)}), bf16[2,16,2048]{2,0,1:T(2,128)(2,1)S(1)}, u32[]{:S(2)}, u32[]{:S(2)}) %all-to-all-start.5) | async-done | bytes 131104 | tf_op jit(solution)/shard_map/all_to_all | solution.py:31
  78.8 3.4 %all-to-all-start.6 = ((bf16[2,16,2048]{2,1,0:T(8,128)(2,1)}), bf16[2,16,2048]{2,1,0:T(8,128)(2,1)S(1)}, u32[]{:S(2)}, u32[]{:S(2)}) async-start(bf16[2,16,2048]{2,1,0:T(8,128)(2,1)} %bitcast.17), calls=%async_computation.6 | async-start | bytes 262144 | tf_op jit(solution)/shard_map/all_to_all | solution.py:40
  82.2 3.3 %all-to-all-done.6 = bf16[2,16,2048]{2,1,0:T(8,128)(2,1)S(1)} async-done(((bf16[2,16,2048]{2,1,0:T(8,128)(2,1)}), bf16[2,16,2048]{2,1,0:T(8,128)(2,1)S(1)}, u32[]{:S(2)}, u32[]{:S(2)}) %all-to-all-start.6) | async-done | bytes 131104 | tf_op jit(solution)/shard_map/all_to_all | solution.py:40
  86.2 5.6 %all-to-all-start.7 = ((bf16[2,16,2048]{2,0,1:T(2,128)(2,1)}), bf16[2,16,2048]{2,0,1:T(2,128)(2,1)S(1)}, u32[]{:S(2)}, u32[]{:S(2)}) async-start(bf16[2,16,2048]{2,0,1:T(2,128)(2,1)} %copy.110), calls=%async_computation.7 | async-start | bytes 262144 | tf_op jit(solution)/shard_map/all_to_all | solution.py:39
  91.9 6.9 %all-to-all-done.7 = bf16[2,16,2048]{2,0,1:T(2,128)(2,1)S(1)} async-done(((bf16[2,16,2048]{2,0,1:T(2,128)(2,1)}), bf16[2,16,2048]{2,0,1:T(2,128)(2,1)S(1)}, u32[]{:S(2)}, u32[]{:S(2)}) %all-to-all-start.7) | async-done | bytes 131104 | tf_op jit(solution)/shard_map/all_to_all | solution.py:39
  98.9 1.8 fusion.28
  100.7 1.1 copy.129
  102.6 2.2 %bitcast_subtract_fusion.2 = (f32[1024,256]{0,1:T(8,128)}, f32[256,1024]{1,0:T(8,128)}) fusion(f32[1024,256]{0,1:T(8,128)S(1)} %get-tuple-element.27, f32[32,8,8,128]{3,2,1,0:T(8,128)S(1)} %bitcast.162, bf16[1,1,1024,1024]{3,2,1,0:T(8,128)(2,1)S(1)} %copy-done), kind=kOutput, calls=%fused_computation.28 | convolution fusion | flops 538181632 | bytes 6291456 | tf_op jit(solution)/shard_map/dot_general | solution.py:63
  104.9 1.4 copy.137
  107.0 5.7 %all_to_all.83 = bf16[2,16,2048]{2,1,0:T(8,128)(2,1)S(1)} all-to-all(bf16[2,16,2048]{2,1,0:T(8,128)(2,1)S(1)} %convert_element_type.86), channel_id=1, replica_groups=mesh['region'=2,'sub'=16] {'region'}, dimensions={0} | all-to-all | bytes 262144 | tf_op jit(solution)/shard_map/all_to_all | solution.py:32
  112.7 0.8 copy.115
  113.5 5.6 %all-to-all-start.9 = ((bf16[2,16,2048]{2,0,1:T(2,128)(2,1)}), bf16[2,16,2048]{2,0,1:T(2,128)(2,1)S(1)}, u32[]{:S(2)}, u32[]{:S(2)}) async-start(bf16[2,16,2048]{2,0,1:T(2,128)(2,1)} %copy.115), calls=%async_computation.9 | async-start | bytes 262144 | tf_op jit(solution)/shard_map/all_to_all | solution.py:31
  119.1 6.9 %all-to-all-done.9 = bf16[2,16,2048]{2,0,1:T(2,128)(2,1)S(1)} async-done(((bf16[2,16,2048]{2,0,1:T(2,128)(2,1)}), bf16[2,16,2048]{2,0,1:T(2,128)(2,1)S(1)}, u32[]{:S(2)}, u32[]{:S(2)}) %all-to-all-start.9) | async-done | bytes 131104 | tf_op jit(solution)/shard_map/all_to_all | solution.py:31
  126.9 5.7 %all_to_all.84 = bf16[2,16,2048]{2,1,0:T(8,128)(2,1)S(1)} all-to-all(bf16[2,16,2048]{2,1,0:T(8,128)(2,1)S(1)} %bitcast.173), channel_id=1, replica_groups=mesh['region'=2,'sub'=16] {'region'}, dimensions={0} | all-to-all | bytes 262144 | tf_op jit(solution)/shard_map/all_to_all | solution.py:40
  133.3 5.6 %all-to-all-start.11 = ((bf16[2,16,2048]{2,0,1:T(2,128)(2,1)}), bf16[2,16,2048]{2,0,1:T(2,128)(2,1)S(1)}, u32[]{:S(2)}, u32[]{:S(2)}) async-start(bf16[2,16,2048]{2,0,1:T(2,128)(2,1)} %copy.117), calls=%async_computation.11 | async-start | bytes 262144 | tf_op jit(solution)/shard_map/all_to_all | solution.py:39
  139.0 6.9 %all-to-all-done.11 = bf16[2,16,2048]{2,0,1:T(2,128)(2,1)S(1)} async-done(((bf16[2,16,2048]{2,0,1:T(2,128)(2,1)}), bf16[2,16,2048]{2,0,1:T(2,128)(2,1)S(1)}, u32[]{:S(2)}, u32[]{:S(2)}) %all-to-all-start.11) | async-done | bytes 131104 | tf_op jit(solution)/shard_map/all_to_all | solution.py:39
  146.0 1.1 fusion.26
  148.1 3.4 %bitcast_subtract_fusion.1 = (f32[1024,256]{0,1:T(8,128)S(1)}, f32[256,1024]{1,0:T(8,128)}) fusion(f32[1024,256]{0,1:T(8,128)} %get-tuple-element.29, f32[32,8,8,128]{3,2,1,0:T(8,128)S(1)} %bitcast.163, bf16[1,1,1024,1024]{3,2,1,0:T(8,128)(2,1)S(1)} %copy-done), kind=kOutput, calls=%fused_computation.27 | convolution fusion | flops 538181632 | bytes 6291456 | tf_op jit(solution)/shard_map/dot_general | solution.py:63
  151.5 1.0 copy.139
  152.5 1.6 gather_fusion.6
  154.3 5.7 %all_to_all.85 = bf16[2,16,2048]{2,1,0:T(8,128)(2,1)S(1)} all-to-all(bf16[2,16,2048]{2,1,0:T(8,128)(2,1)S(1)} %convert_element_type.89), channel_id=1, replica_groups=mesh['region'=2,'sub'=16] {'region'}, dimensions={0} | all-to-all | bytes 262144 | tf_op jit(solution)/shard_map/all_to_all | solution.py:32
  160.8 5.6 %all-to-all-start.13 = ((bf16[2,16,2048]{2,0,1:T(2,128)(2,1)}), bf16[2,16,2048]{2,0,1:T(2,128)(2,1)S(1)}, u32[]{:S(2)}, u32[]{:S(2)}) async-start(bf16[2,16,2048]{2,0,1:T(2,128)(2,1)} %copy.122), calls=%async_computation.13 | async-start | bytes 262144 | tf_op jit(solution)/shard_map/all_to_all | solution.py:31
  166.4 6.9 %all-to-all-done.13 = bf16[2,16,2048]{2,0,1:T(2,128)(2,1)S(1)} async-done(((bf16[2,16,2048]{2,0,1:T(2,128)(2,1)}), bf16[2,16,2048]{2,0,1:T(2,128)(2,1)S(1)}, u32[]{:S(2)}, u32[]{:S(2)}) %all-to-all-start.13) | async-done | bytes 131104 | tf_op jit(solution)/shard_map/all_to_all | solution.py:31
  174.1 5.7 %all_to_all.86 = bf16[2,16,2048]{2,1,0:T(8,128)(2,1)S(1)} all-to-all(bf16[2,16,2048]{2,1,0:T(8,128)(2,1)S(1)} %bitcast.174), channel_id=1, replica_groups=mesh['region'=2,'sub'=16] {'region'}, dimensions={0} | all-to-all | bytes 262144 | tf_op jit(solution)/shard_map/all_to_all | solution.py:40
  180.0 11.7 %all_to_all.87 = bf16[2,16,2048]{2,0,1:T(2,128)(2,1)S(1)} all-to-all(bf16[2,16,2048]{2,0,1:T(2,128)(2,1)S(1)} %copy.124), channel_id=1, replica_groups=mesh['region'=2,'sub'=16] {'sub'}, dimensions={1} | all-to-all | bytes 262144 | tf_op jit(solution)/shard_map/all_to_all | solution.py:39
  191.7 1.8 fusion.24
  193.6 1.1 copy.133
  197.3 20.5 %all_gather.3 = bf16[1024,256]{1,0:T(8,128)(2,1)S(1)} all-gather(bf16[64,256]{1,0:T(8,128)(2,1)S(1)} %fusion.10), channel_id=1, replica_groups=mesh['region'=2,'sub'=16] {'sub'}, dimensions={0}, use_global_device_ids=true | all-gather | bytes 557056 | tf_op jit(solution)/shard_map/all_gather | solution.py:74
  217.8 2.8 %fusion.9 = bf16[1,1,1024,256]{2,3,1,0:T(8,128)(2,1)S(1)} fusion(bf16[1024,256]{1,0:T(8,128)(2,1)S(1)} %all_gather.3, f32[256,1024]{1,0:T(8,128)} %copy-done.1, f32[256,1024]{1,0:T(8,128)} %get-tuple-element.32, f32[256,1024]{1,0:T(8,128)} %get-tuple-element.28, f32[256,1024]{1,0:T(8,128)} %get-tuple-element.30, bf16[1,64,1024]{2,1,0:T(8,128)(2,1)S(1)} %copy-done.3, ...), kind=kOutput, calls=%fused_computation.18 | convolution fusion | flops 68435968 | bytes 5505024 | tf_op jit(solution)/shard_map/dot_general | solution.py:77
  220.6 1.0 copy.128
  (67 shorter events, 15.6 us)
Async XLA Ops:
  0.0 52.2 %copy-start = (bf16[1,1,1024,1024]{3,2,1,0:T(8,128)(2,1)S(1)}, bf16[1,1,1024,1024]{3,2,1,0:T(8,128)(2,1)}, u32[]{:S(2)}) copy-start(bf16[1,1,1024,1024]{3,2,1,0:T(8,128)(2,1)} %param.12) | copy-start | bytes 6291460
  1.1 19.2 %copy-start.4 = (s32[4,32]{1,0:T(4,128)S(1)}, s32[4,32]{1,0:T(4,128)}, u32[]{:S(2)}) copy-start(s32[4,32]{1,0:T(4,128)} %param.15) | copy-start | bytes 1540
  12.4 14.8 %all-to-all-start.1 = ((bf16[2,16,2048]{2,0,1:T(2,128)(2,1)}), bf16[2,16,2048]{2,0,1:T(2,128)(2,1)S(1)}, u32[]{:S(2)}, u32[]{:S(2)}) async-start(bf16[2,16,2048]{2,0,1:T(2,128)(2,1)} %copy.98), calls=%async_computation.1 | async-start | bytes 262144 | tf_op jit(solution)/shard_map/all_to_all | solution.py:31
  34.5 12.6 %all-to-all-start.3 = ((bf16[2,16,2048]{2,0,1:T(2,128)(2,1)}), bf16[2,16,2048]{2,0,1:T(2,128)(2,1)S(1)}, u32[]{:S(2)}, u32[]{:S(2)}) async-start(bf16[2,16,2048]{2,0,1:T(2,128)(2,1)} %copy.100), calls=%async_computation.3 | async-start | bytes 262144 | tf_op jit(solution)/shard_map/all_to_all | solution.py:39
  64.8 12.6 %all-to-all-start.5 = ((bf16[2,16,2048]{2,0,1:T(2,128)(2,1)}), bf16[2,16,2048]{2,0,1:T(2,128)(2,1)S(1)}, u32[]{:S(2)}, u32[]{:S(2)}) async-start(bf16[2,16,2048]{2,0,1:T(2,128)(2,1)} %copy.108), calls=%async_computation.5 | async-start | bytes 262144 | tf_op jit(solution)/shard_map/all_to_all | solution.py:31
  78.8 6.7 %all-to-all-start.6 = ((bf16[2,16,2048]{2,1,0:T(8,128)(2,1)}), bf16[2,16,2048]{2,1,0:T(8,128)(2,1)S(1)}, u32[]{:S(2)}, u32[]{:S(2)}) async-start(bf16[2,16,2048]{2,1,0:T(8,128)(2,1)} %bitcast.17), calls=%async_computation.6 | async-start | bytes 262144 | tf_op jit(solution)/shard_map/all_to_all | solution.py:40
  86.2 12.6 %all-to-all-start.7 = ((bf16[2,16,2048]{2,0,1:T(2,128)(2,1)}), bf16[2,16,2048]{2,0,1:T(2,128)(2,1)S(1)}, u32[]{:S(2)}, u32[]{:S(2)}) async-start(bf16[2,16,2048]{2,0,1:T(2,128)(2,1)} %copy.110), calls=%async_computation.7 | async-start | bytes 262144 | tf_op jit(solution)/shard_map/all_to_all | solution.py:39
  113.5 12.6 %all-to-all-start.9 = ((bf16[2,16,2048]{2,0,1:T(2,128)(2,1)}), bf16[2,16,2048]{2,0,1:T(2,128)(2,1)S(1)}, u32[]{:S(2)}, u32[]{:S(2)}) async-start(bf16[2,16,2048]{2,0,1:T(2,128)(2,1)} %copy.115), calls=%async_computation.9 | async-start | bytes 262144 | tf_op jit(solution)/shard_map/all_to_all | solution.py:31
  133.3 12.6 %all-to-all-start.11 = ((bf16[2,16,2048]{2,0,1:T(2,128)(2,1)}), bf16[2,16,2048]{2,0,1:T(2,128)(2,1)S(1)}, u32[]{:S(2)}, u32[]{:S(2)}) async-start(bf16[2,16,2048]{2,0,1:T(2,128)(2,1)} %copy.117), calls=%async_computation.11 | async-start | bytes 262144 | tf_op jit(solution)/shard_map/all_to_all | solution.py:39
  160.8 12.6 %all-to-all-start.13 = ((bf16[2,16,2048]{2,0,1:T(2,128)(2,1)}), bf16[2,16,2048]{2,0,1:T(2,128)(2,1)S(1)}, u32[]{:S(2)}, u32[]{:S(2)}) async-start(bf16[2,16,2048]{2,0,1:T(2,128)(2,1)} %copy.122), calls=%async_computation.13 | async-start | bytes 262144 | tf_op jit(solution)/shard_map/all_to_all | solution.py:31
  195.4 0.9 copy-start.2
  196.3 1.0 copy-start.1
  196.3 21.4 %copy-start.3 = (bf16[1,64,1024]{2,1,0:T(8,128)(2,1)S(1)}, bf16[1,64,1024]{2,1,0:T(8,128)(2,1)}, u32[]{:S(2)}) copy-start(bf16[1,64,1024]{2,1,0:T(8,128)(2,1)} %param.17) | copy-start | bytes 393220
where the time goes:
time: 223 us; the launch traced here: 222 us
  blocking collectives  72.8 us (33%)
  waiting for transfers between devices  51.8 us (23%)
  starting transfers between devices  45 us (20%)
  local copies, waits for them, and re-layouts  27.8 us (12%)
  matrix products  22.5 us (10%)
    all_to_all x4, waiting for transfers between devices, shards(): lax.all_to_all(lax.all_to_all(pieces, 'region', split_axis=0, concat_axis...  27.7 us
    all_to_all x4, starting transfers between devices, shards(): lax.all_to_all(lax.all_to_all(pieces, 'region', split_axis=0, concat_axis...  24.8 us
    all_to_all x4, blocking collectives, shards(): lax.all_to_all(pieces, 'region', split_axis=0, concat_axis=0, tiled=True)  23.5 us
    all_to_all x3, waiting for transfers between devices, shards(): lax.all_to_all(lax.all_to_all(relayed.reshape(region_peers, sub_peers, pi...  20.8 us
    all_gather x1, blocking collectives, shards(): lax.all_gather(projected, 'sub', axis=0, tiled=True)  20.5 us
    all_to_all x3, blocking collectives, shards(): lax.all_to_all(relayed.reshape(region_peers, sub_peers, piece_len), 'regi...  17.1 us
    all_to_all x3, starting transfers between devices, shards(): lax.all_to_all(lax.all_to_all(relayed.reshape(region_peers, sub_peers, pi...  16.8 us
    all_to_all x1, blocking collectives, shards(): lax.all_to_all(lax.all_to_all(relayed.reshape(region_peers, sub_peers, pi...  11.7 us
  transfers between devices with their start and end apart: 8, of which 8 were waited for; matrix products, arithmetic and copies ran while one was open for 0% of the time, Pallas kernels for 0%

commit v1 on v0

v1 whole, which is shorter than its diff:
```python
import functools

import jax
import jax.numpy as jnp
from jax import lax
from jax.experimental import pallas as pl
from jax.experimental.pallas import tpu as pltpu
from jax.sharding import PartitionSpec as P

BLK = 128
OVL_BLK = 2
COLORS = 4
TILE_ROWS = 16
TILE_COLS = 128
MESH = pl.DeviceIdType.MESH


def sweep(
    regions,
    subs,
    right_ref,
    inverse_ref,
    coupling_ref,
    blocks_ref,
    partner_ref,
    restriction_ref,
    coarse_ref,
    out_ref,
    residual,
    accumulated,
    shaped,
    outgoing,
    arrived,
    forwarded,
    received,
    stacked,
    sem_spread_out,
    sem_spread_in,
    sem_back_out,
    sem_back_in,
    sem_gather_out,
    sem_gather_in,
    sem_pair_out,
    sem_pair_in,
):
    count = regions * subs
    region, sub = lax.axis_index("region"), lax.axis_index("sub")
    me = region * subs + sub
    block_count, _, columns = right_ref.shape
    rows = block_count * BLK
    span = OVL_BLK * BLK
    row_tiles, col_tiles = span // TILE_ROWS, columns // TILE_COLS
    pieces = row_tiles * col_tiles
    stride = count // pieces
    slot = me // stride
    is_relay = lax.rem(me, stride) == 0
    cp = restriction_ref.shape[0]

    def place(number):
        return (number // subs, lax.rem(number, subs))

    barrier = pltpu.get_barrier_semaphore()

    def greet(step, carry):
        other = lax.rem(me + step, count)
        pl.semaphore_signal(barrier, inc=1, device_id=place(other), device_id_type=MESH)
        return carry

    lax.fori_loop(1, count, greet, 0)

    def spread_copy(colour, piece):
        return pltpu.make_async_remote_copy(
            src_ref=outgoing.at[colour, piece],
            dst_ref=arrived[colour].at[me],
            send_sem=sem_spread_out.at[colour],
            recv_sem=sem_spread_in.at[colour],
            device_id=place(piece * stride),
            device_id_type=MESH,
        )

    def back_copy(colour, owner):
        return pltpu.make_async_remote_copy(
            src_ref=forwarded.at[colour, owner],
            dst_ref=received.at[colour, slot],
            send_sem=sem_back_out.at[colour],
            recv_sem=sem_back_in.at[colour],
            device_id=place(owner),
            device_id_type=MESH,
        )

    def wait_bytes(buffer, number, sem):
        view = buffer.at[pl.ds(0, number)]
        pltpu.make_async_copy(view, view, sem).wait()

    def on_relay(body):
        if stride == 1:
            body()
        else:
            pl.when(is_relay)(body)

    def off_relay(body):
        if stride > 1:
            pl.when(jnp.logical_not(is_relay))(body)

    def spread(colour, k, values):
        half = BLK // TILE_ROWS
        for col in range(col_tiles):
            block = values[:, col * TILE_COLS : (col + 1) * TILE_COLS]
            first = col * row_tiles + k * half
            outgoing[colour, first : first + half] = block.reshape(half, TILE_ROWS, TILE_COLS)

    def start_spread(colour):
        def send(step, carry):
            spread_copy(colour, lax.rem(slot + step, pieces)).start()
            return carry

        lax.fori_loop(1, pieces, send, 0)

        @on_relay
        def _():
            arrived[colour][me] = outgoing[colour, slot]

        @off_relay
        def _():
            spread_copy(colour, slot).start()

    def relay(colour):
        @on_relay
        def _():
            wait_bytes(arrived[colour], count - 1, sem_spread_in.at[colour])

            def send(step, carry):
                owner = lax.rem(me + step, count)
                forwarded[colour, owner] = arrived[colour][partner_ref[colour, owner]]
                back_copy(colour, owner).start()
                return carry

            lax.fori_loop(1, count, send, 0)
            received[colour, slot] = arrived[colour][partner_ref[colour, me]]

    def collect(colour):
        @on_relay
        def _():
            wait_bytes(received.at[colour], pieces - 1, sem_back_in.at[colour])

        @off_relay
        def _():
            wait_bytes(received.at[colour], pieces, sem_back_in.at[colour])

    for k in range(OVL_BLK):
        spread(0, k, right_ref[blocks_ref[0, k]])
    pl.semaphore_wait(barrier, count - 1)
    start_spread(0)
    residual[...] = right_ref[...].astype(jnp.float32)

    for colour in range(COLORS):
        relay(colour)
        collect(colour)
        got = received[colour]
        got = jnp.concatenate(
            [
                got[c * row_tiles : (c + 1) * row_tiles].reshape(span, TILE_COLS)
                for c in range(col_tiles)
            ],
            axis=1,
        )
        coupled = jnp.dot(coupling_ref[colour], got, preferred_element_type=jnp.float32)
        for b in range(block_count):
            wide = residual[b]
            for k in range(OVL_BLK):
                apart = blocks_ref[colour, k] - b
                chosen = (1 - jnp.minimum(apart * apart, 1)).astype(jnp.float32)
                wide = wide + chosen * coupled[k * BLK : (k + 1) * BLK]
            residual[b] = wide
            shaped[b * BLK : (b + 1) * BLK, :] = wide.astype(jnp.bfloat16)
        if colour + 1 < COLORS:
            for k in range(OVL_BLK):
                block = blocks_ref[colour + 1, k]
                fix = jnp.dot(
                    inverse_ref[block], shaped[...], preferred_element_type=jnp.float32
                )
                left = residual[block] - 0.25 * fix
                spread(colour + 1, k, left.astype(jnp.bfloat16))
            start_spread(colour + 1)
        for b in range(0, block_count, 2):
            fix = jnp.dot(
                inverse_ref[b : b + 2].reshape(2 * BLK, rows),
                shaped[...],
                preferred_element_type=jnp.float32,
            ).reshape(2, BLK, columns)
            if colour == 0:
                accumulated[b : b + 2] = fix
            else:
                accumulated[b : b + 2] = accumulated[b : b + 2] + fix
            residual[b : b + 2] = residual[b : b + 2] - 0.25 * fix

    projected = jnp.dot(
        restriction_ref[...],
        residual[...].astype(jnp.bfloat16).reshape(rows, columns),
        preferred_element_type=jnp.float32,
    )
    stacked[sub] = projected.astype(jnp.bfloat16)

    chips = subs // 2
    core = lax.rem(sub, 2)
    mate = sub + 1 - 2 * core

    def gather_copy(step):
        return pltpu.make_async_remote_copy(
            src_ref=stacked.at[sub],
            dst_ref=stacked.at[sub],
            send_sem=sem_gather_out.at[step],
            recv_sem=sem_gather_in.at[step],
            device_id=(region, lax.rem(sub + 2 * step, subs)),
            device_id_type=MESH,
        )

    def pair_copy(step):
        from_sub = lax.rem(sub + subs - 2 * step, subs)
        return pltpu.make_async_remote_copy(
            src_ref=stacked.at[from_sub],
            dst_ref=stacked.at[from_sub],
            send_sem=sem_pair_out.at[step],
            recv_sem=sem_pair_in.at[step],
            device_id=(region, mate),
            device_id_type=MESH,
        )

    for step in range(1, chips):
        gather_copy(step).start()
    pair_copy(0).start()
    for step in range(1, chips):
        gather_copy(step).wait_recv()
        pair_copy(step).start()
    for step in range(chips):
        pair_copy(step).wait_recv()
    everything = stacked[...].reshape(subs * cp, columns)
    coarse = jnp.dot(coarse_ref[...], everything, preferred_element_type=jnp.float32)
    coarse = coarse.astype(jnp.bfloat16)
    lifted = lax.dot_general(
        restriction_ref[...], coarse, (((0,), (0,)), ((), ())), preferred_element_type=jnp.float32
    )
    lifted = lifted.reshape(block_count, BLK, columns)
    out_ref[...] = (accumulated[...] + lifted).astype(jnp.bfloat16)

    for step in range(1, chips):
        gather_copy(step).wait_send()
    for step in range(chips):
        pair_copy(step).wait_send()
    for colour in range(COLORS):

        @on_relay
        def _():
            wait_bytes(outgoing.at[colour], pieces - 1, sem_spread_out.at[colour])
            wait_bytes(forwarded.at[colour], count - 1, sem_back_out.at[colour])

        @off_relay
        def _():
            wait_bytes(outgoing.at[colour], pieces, sem_spread_out.at[colour])


def shards(right_side, local_inverse, coupling, margin_blocks, partner, restriction, coarse_rows):
    regions, subs = lax.axis_size("region"), lax.axis_size("sub")
    count = regions * subs
    right = right_side[0, 0]
    rows, columns = right.shape
    pieces = OVL_BLK * BLK * columns // (TILE_ROWS * TILE_COLS)
    cp = restriction.shape[2]
    piece = (TILE_ROWS, TILE_COLS)
    blocked = (rows // BLK, BLK, columns)
    vmem = pl.BlockSpec(memory_space=pltpu.VMEM)
    smem = pl.BlockSpec(memory_space=pltpu.SMEM)
    dma = pltpu.SemaphoreType.DMA
    result = pl.pallas_call(
        functools.partial(sweep, regions, subs),
        out_shape=jax.ShapeDtypeStruct(blocked, jnp.bfloat16),
        in_specs=[vmem, vmem, vmem, smem, smem, vmem, vmem],
        out_specs=vmem,
        scratch_shapes=[
            pltpu.VMEM(blocked, jnp.float32),
            pltpu.VMEM(blocked, jnp.float32),
            pltpu.VMEM((rows, columns), jnp.bfloat16),
            pltpu.VMEM((COLORS, pieces) + piece, jnp.bfloat16),
            [pltpu.VMEM((count,) + piece, jnp.bfloat16) for _ in range(COLORS)],
            pltpu.VMEM((COLORS, count) + piece, jnp.bfloat16),
            pltpu.VMEM((COLORS, pieces) + piece, jnp.bfloat16),
            pltpu.VMEM((subs, cp, columns), jnp.bfloat16),
            dma((COLORS,)),
            dma((COLORS,)),
            dma((COLORS,)),
            dma((COLORS,)),
            dma((subs // 2,)),
            dma((subs // 2,)),
            dma((subs // 2,)),
            dma((subs // 2,)),
        ],
        compiler_params=pltpu.CompilerParams(
            collective_id=0, has_side_effects=True, vmem_limit_bytes=48 * 1024 * 1024
        ),
    )(
        right.reshape(blocked),
        local_inverse.reshape(rows // BLK, BLK, rows),
        coupling[0, 0],
        margin_blocks[:, 0, 0, :],
        partner,
        restriction[0, 0],
        coarse_rows[0],
    )
    return result.reshape(right_side.shape)


def solution(mesh):
    placed = (
        P("region", "sub", None, None),
        P("region", "sub", None, None),
        P("region", "sub", None, None, None),
        P(None, "region", "sub", None),
        P(),
        P("region", "sub", None, None),
        P("region", "sub", None),
    )
    return jax.shard_map(
        shards,
        mesh=mesh,
        in_specs=placed,
        out_specs=P("region", "sub", None, None),
        check_vma=False,
    )
```

time: 223 us -> 69.9 us (0.31)
  blocking collectives: 72.8 us -> 0 us
  Pallas kernels: 0 us -> 61.8 us
  waiting for transfers between devices: 51.8 us -> 0 us
  starting transfers between devices: 45 us -> 0 us
  matrix products: 22.5 us -> 0 us
  local copies, waits for them, and re-layouts: 27.8 us -> 7.72 us
    pallas_call x0 -> x1, Pallas kernels: none -> 61.8 us  [shards(): pl.pallas_call(functools.partial(sweep, regions, subs), out_shape=jax.Sha...]
    all_to_all x8 -> x0, blocking collectives: 52.3 us -> none  [the longest x4 23.5 us: shards(): lax.all_to_all(pieces, 'region', split_axis=0, concat_axis=0, tiled=True)]
    all_to_all x8 -> x0, waiting for transfers between devices: 51.8 us -> none  [the longest x4 27.7 us: shards(): lax.all_to_all(lax.all_to_all(pieces, 'region', split_axis=0, concat_axis...]
    all_to_all x8 -> x0, starting transfers between devices: 45 us -> none  [the longest x4 24.8 us: shards(): lax.all_to_all(lax.all_to_all(pieces, 'region', split_axis=0, concat_axis...]
    dot_general x14 -> x0, matrix products: 22.5 us -> none  [the longest x4 9.76 us: shards(): correction = jnp.dot(inverse, shaped, preferred_element_type=jnp.float32)]
    all_gather x1 -> x0, blocking collectives: 20.5 us -> none  [shards(): lax.all_gather(projected, 'sub', axis=0, tiled=True)]
    reshape x11 -> x0, local copies, waits for them, and re-layouts: 7.35 us -> none  [the longest x3 3.42 us: shards(): tiled = residual.reshape(block_count, BLK, columns)]
    gather x8 -> x0, local copies, waits for them, and re-layouts: 6.91 us -> none  [the longest x4 4.31 us: shards(): jnp.take(tiled, picked, axis=0).reshape(span_rows, columns)]
  transfers between devices with their start and end apart: 8 -> 0, of which waited for: 8 -> 0; matrix products, arithmetic and copies ran while one was open for 0% -> 0% of each run, Pallas kernels for 0% -> 0%
where the time goes in v1:
time: 69.9 us; the launch traced here: 69.6 us
  Pallas kernels  61.8 us (88%)
  local copies, waits for them, and re-layouts  7.72 us (11%)
    pallas_call x1, Pallas kernels, shards(): pl.pallas_call(functools.partial(sweep, regions, subs), out_shape=jax.Sha...  61.8 us
    unnamed x13, local copies, waits for them, and re-layouts  6.96 us

profile of v1, /device:TPU:1, one launch (start us, length us, event | category | flops | bytes accessed | tf_op | source)
XLA Modules:
  0.0 69.6 jit_solution(3723109440933953397)
XLA Ops:
  0.0 0.8 %copy.8.blocks_ref = s32[4,2]{1,0:T(4,128)S(1)} copy(s32[4,2]{0,1:T(2,128)} %bitcast.13) | data formatting | bytes 64 | tf_op jit(solution)/shard_map/squeeze | solution.py:304
  0.8 0.0 copy-start
  0.8 1.6 %copy-done = bf16[1,1,1024,1024]{3,2,1,0:T(8,128)(2,1)S(1)} copy-done((bf16[1,1,1024,1024]{3,2,1,0:T(8,128)(2,1)S(1)}, bf16[1,1,1024,1024]{3,2,1,0:T(8,128)(2,1)}, u32[]{:S(2)}) %copy-start) | copy-done | bytes 2097176
  2.4 0.0 copy-start.1
  2.4 1.0 %copy-done.1 = bf16[1,1,1024,256]{3,2,1,0:T(8,128)(2,1)S(1)} copy-done((bf16[1,1,1024,256]{3,2,1,0:T(8,128)(2,1)S(1)}, bf16[1,1,1024,256]{3,2,1,0:T(8,128)(2,1)}, u32[]{:S(2)}) %copy-start.1) | copy-done | bytes 524312
  3.4 0.0 copy-start.2
  3.4 1.0 %copy-done.2 = bf16[1,1,4,256,256]{4,3,2,1,0:T(8,128)(2,1)S(1)} copy-done((bf16[1,1,4,256,256]{4,3,2,1,0:T(8,128)(2,1)S(1)}, bf16[1,1,4,256,256]{4,3,2,1,0:T(8,128)(2,1)}, u32[]{:S(2)}) %copy-start.2) | copy-done | bytes 524312
  4.4 0.0 copy-start.3
  4.4 0.9 %copy-done.3 = bf16[1,1,64,1024]{3,2,1,0:T(8,128)(2,1)S(1)} copy-done((bf16[1,1,64,1024]{3,2,1,0:T(8,128)(2,1)S(1)}, bf16[1,1,64,1024]{3,2,1,0:T(8,128)(2,1)}, u32[]{:S(2)}) %copy-start.3) | copy-done | bytes 131096
  5.3 0.0 copy-start.4
  5.3 0.9 %copy-done.4 = bf16[1,64,1024]{2,1,0:T(8,128)(2,1)S(1)} copy-done((bf16[1,64,1024]{2,1,0:T(8,128)(2,1)S(1)}, bf16[1,64,1024]{2,1,0:T(8,128)(2,1)}, u32[]{:S(2)}) %copy-start.4) | copy-done | bytes 131096
  6.3 0.0 copy-start.5
  6.3 0.7 copy-done.5
  6.9 61.8 %shard_map.73 = bf16[8,128,256]{2,1,0:T(8,128)(2,1)S(1)} custom-call(bf16[8,128,256]{2,1,0:T(8,128)(2,1)S(1)} %bitcast.9, bf16[8,128,1024]{2,1,0:T(8,128)(2,1)S(1)} %bitcast.8, bf16[4,256,256]{2,1,0:T(8,128)(2,1)S(1)} %bitcast.10, s32[4,2]{1,0:T(4,128)S(1)} %copy.8.blocks_ref, s32[4,32]{1,0:T(4,128)S(1)} %copy-done.5, bf16[64,1024]{1,0:T(8,128)(2,1)S(1)} %bitcast.11, ...), custom_call_target="tpu_custom_call" | custom-call | tf_op jit(solution)/shard_map/pallas_call | solution.py:274
  68.8 0.8 %copy.10 = bf16[1,1,1024,256]{3,2,1,0:T(8,128)(2,1)} copy(bf16[1,1,1024,256]{3,2,1,0:T(8,128)(2,1)S(1)} %bitcast.7) | data formatting | bytes 1048576
Async XLA Ops:
  0.8 1.6 %copy-start = (bf16[1,1,1024,1024]{3,2,1,0:T(8,128)(2,1)S(1)}, bf16[1,1,1024,1024]{3,2,1,0:T(8,128)(2,1)}, u32[]{:S(2)}) copy-start(bf16[1,1,1024,1024]{3,2,1,0:T(8,128)(2,1)} %param.8) | copy-start | bytes 6291460
  2.4 1.0 %copy-start.1 = (bf16[1,1,1024,256]{3,2,1,0:T(8,128)(2,1)S(1)}, bf16[1,1,1024,256]{3,2,1,0:T(8,128)(2,1)}, u32[]{:S(2)}) copy-start(bf16[1,1,1024,256]{3,2,1,0:T(8,128)(2,1)} %param.7) | copy-start | bytes 1572868
  3.4 1.0 %copy-start.2 = (bf16[1,1,4,256,256]{4,3,2,1,0:T(8,128)(2,1)S(1)}, bf16[1,1,4,256,256]{4,3,2,1,0:T(8,128)(2,1)}, u32[]{:S(2)}) copy-start(bf16[1,1,4,256,256]{4,3,2,1,0:T(8,128)(2,1)} %param.9) | copy-start | bytes 1572868
  4.4 0.9 %copy-start.3 = (bf16[1,1,64,1024]{3,2,1,0:T(8,128)(2,1)S(1)}, bf16[1,1,64,1024]{3,2,1,0:T(8,128)(2,1)}, u32[]{:S(2)}) copy-start(bf16[1,1,64,1024]{3,2,1,0:T(8,128)(2,1)} %param.12) | copy-start | bytes 393220
  5.3 0.9 %copy-start.4 = (bf16[1,64,1024]{2,1,0:T(8,128)(2,1)S(1)}, bf16[1,64,1024]{2,1,0:T(8,128)(2,1)}, u32[]{:S(2)}) copy-start(bf16[1,64,1024]{2,1,0:T(8,128)(2,1)} %param.13) | copy-start | bytes 393220
  6.3 0.7 copy-start.5

commit v2 on v1

v2 whole, which is shorter than its diff:
```python
import functools

import jax
import jax.numpy as jnp
from jax import lax
from jax.experimental import pallas as pl
from jax.experimental.pallas import tpu as pltpu
from jax.sharding import PartitionSpec as P

BLK = 128
OVL_BLK = 2
COLORS = 4
TILE_ROWS = 16
TILE_COLS = 128
UNROLL = False
MESH = pl.DeviceIdType.MESH


def sweep(
    regions,
    subs,
    right_hbm,
    inverse_hbm,
    coupling_hbm,
    blocks_ref,
    partner_ref,
    restriction_hbm,
    coarse_hbm,
    out_ref,
    right_ref,
    inverse_ref,
    coupling_ref,
    restriction_ref,
    coarse_ref,
    sem_load,
    residual,
    accumulated,
    shaped,
    outgoing,
    arrived,
    forwarded,
    received,
    stacked,
    sem_spread_out,
    sem_spread_in,
    sem_back_out,
    sem_back_in,
    sem_gather_out,
    sem_gather_in,
    sem_pair_out,
    sem_pair_in,
):
    count = regions * subs
    region, sub = lax.axis_index("region"), lax.axis_index("sub")
    me = region * subs + sub
    block_count, _, columns = right_hbm.shape
    rows = block_count * BLK
    span = OVL_BLK * BLK
    row_tiles, col_tiles = span // TILE_ROWS, columns // TILE_COLS
    pieces = row_tiles * col_tiles
    stride = count // pieces
    slot = me // stride
    my_half, my_tile = lax.rem(slot, col_tiles), slot // col_tiles
    my_piece = my_half * row_tiles + my_tile
    is_relay = lax.rem(me, stride) == 0
    cp = restriction_hbm.shape[0]

    def place(number):
        return (number // subs, lax.rem(number, subs))

    loads = [
        pltpu.make_async_copy(source, target, sem_load.at[i])
        for i, (source, target) in enumerate(
            [
                (right_hbm, right_ref),
                (coupling_hbm, coupling_ref),
                (inverse_hbm, inverse_ref),
                (restriction_hbm, restriction_ref),
                (coarse_hbm, coarse_ref),
            ]
        )
    ]
    for load in loads:
        load.start()

    barrier = pltpu.get_barrier_semaphore()

    def greet(step, carry):
        other = lax.rem(me + step, count)
        pl.semaphore_signal(barrier, inc=1, device_id=place(other), device_id_type=MESH)
        return carry

    lax.fori_loop(1, count, greet, 0)

    def spread_copy(colour, half, tile):
        piece = half * row_tiles + tile
        return pltpu.make_async_remote_copy(
            src_ref=outgoing.at[colour, piece],
            dst_ref=arrived[colour].at[me],
            send_sem=sem_spread_out.at[colour],
            recv_sem=sem_spread_in.at[colour],
            device_id=place((tile * col_tiles + half) * stride),
            device_id_type=MESH,
        )

    def back_copy(colour, owner):
        return pltpu.make_async_remote_copy(
            src_ref=forwarded.at[colour, owner],
            dst_ref=received.at[colour, my_piece],
            send_sem=sem_back_out.at[colour],
            recv_sem=sem_back_in.at[colour, my_half],
            device_id=place(owner),
            device_id_type=MESH,
        )

    def wait_bytes(buffer, number, sem):
        view = buffer.at[pl.ds(0, number)]
        pltpu.make_async_copy(view, view, sem).wait()

    def on_relay(body):
        if stride == 1:
            body()
        else:
            pl.when(is_relay)(body)

    def off_relay(body):
        if stride > 1:
            pl.when(jnp.logical_not(is_relay))(body)

    def own_half(half):
        if stride == 1:
            return my_half == half
        return jnp.logical_and(is_relay, my_half == half)

    def lanes(half):
        return slice(half * TILE_COLS, (half + 1) * TILE_COLS)

    def spread(colour, half, k, values):
        tiles = BLK // TILE_ROWS
        first = half * row_tiles + k * tiles
        outgoing[colour, first : first + tiles] = values.reshape(tiles, TILE_ROWS, TILE_COLS)

    def start_spread(colour, half):
        def send(step, carry):
            spread_copy(colour, half, lax.rem(my_tile + step, row_tiles)).start()
            return carry

        lax.fori_loop(1, row_tiles, send, 0, unroll=UNROLL)

        @pl.when(own_half(half))
        def _():
            arrived[colour][me] = outgoing[colour, my_piece]

        @pl.when(jnp.logical_not(own_half(half)))
        def _():
            spread_copy(colour, half, my_tile).start()

    def relay(colour):
        @on_relay
        def _():
            wait_bytes(arrived[colour], count - 1, sem_spread_in.at[colour])

            def send(step, carry):
                owner = lax.rem(me + step, count)
                forwarded[colour, owner] = arrived[colour][partner_ref[colour, owner]]
                back_copy(colour, owner).start()
                return carry

            lax.fori_loop(1, count, send, 0, unroll=UNROLL)
            received[colour, my_piece] = arrived[colour][partner_ref[colour, me]]

    def collect(colour, half):
        @pl.when(own_half(half))
        def _():
            wait_bytes(received.at[colour], row_tiles - 1, sem_back_in.at[colour, half])

        @pl.when(jnp.logical_not(own_half(half)))
        def _():
            wait_bytes(received.at[colour], row_tiles, sem_back_in.at[colour, half])

    def correct(colour, half):
        part = lanes(half)
        for b in range(0, block_count, 2):
            fix = jnp.dot(
                inverse_ref[b : b + 2].reshape(2 * BLK, rows),
                shaped[:, part],
                preferred_element_type=jnp.float32,
            ).reshape(2, BLK, TILE_COLS)
            if colour == 0:
                accumulated[b : b + 2, :, part] = fix
            else:
                accumulated[b : b + 2, :, part] = accumulated[b : b + 2, :, part] + fix
            residual[b : b + 2, :, part] = residual[b : b + 2, :, part] - 0.25 * fix

    chips = subs // 2
    core = lax.rem(sub, 2)
    mate = sub + 1 - 2 * core

    def gather_copy(half, step):
        return pltpu.make_async_remote_copy(
            src_ref=stacked.at[half, sub],
            dst_ref=stacked.at[half, sub],
            send_sem=sem_gather_out.at[half, step],
            recv_sem=sem_gather_in.at[half, step],
            device_id=(region, lax.rem(sub + 2 * step, subs)),
            device_id_type=MESH,
        )

    def pair_copy(half, step):
        from_sub = lax.rem(sub + subs - 2 * step, subs)
        return pltpu.make_async_remote_copy(
            src_ref=stacked.at[half, from_sub],
            dst_ref=stacked.at[half, from_sub],
            send_sem=sem_pair_out.at[half, step],
            recv_sem=sem_pair_in.at[half, step],
            device_id=(region, mate),
            device_id_type=MESH,
        )

    halves = range(col_tiles)
    loads[0].wait()
    for half in halves:
        for k in range(OVL_BLK):
            spread(0, half, k, right_ref[blocks_ref[k, 0]][:, lanes(half)])
    pl.semaphore_wait(barrier, count - 1)
    for half in halves:
        start_spread(0, half)
    residual[...] = right_ref[...].astype(jnp.float32)
    for load in loads[1:]:
        load.wait()

    for colour in range(COLORS):
        relay(colour)
        for half in halves:
            part = lanes(half)
            collect(colour, half)
            got = received[colour, half * row_tiles : (half + 1) * row_tiles]
            coupled = jnp.dot(
                coupling_ref[colour],
                got.reshape(span, TILE_COLS),
                preferred_element_type=jnp.float32,
            )
            for b in range(block_count):
                wide = residual[b, :, part]
                for k in range(OVL_BLK):
                    apart = blocks_ref[k, colour] - b
                    chosen = (1 - jnp.minimum(apart * apart, 1)).astype(jnp.float32)
                    wide = wide + chosen * coupled[k * BLK : (k + 1) * BLK]
                residual[b, :, part] = wide
                shaped[b * BLK : (b + 1) * BLK, part] = wide.astype(jnp.bfloat16)
            if colour + 1 < COLORS:
                for k in range(OVL_BLK):
                    block = blocks_ref[k, colour + 1]
                    fix = jnp.dot(
                        inverse_ref[block], shaped[:, part], preferred_element_type=jnp.float32
                    )
                    left = residual[block][:, part] - 0.25 * fix
                    spread(colour + 1, half, k, left.astype(jnp.bfloat16))
                start_spread(colour + 1, half)
            else:
                correct(colour, half)
                projected = jnp.dot(
                    restriction_ref[...],
                    residual[:, :, part].astype(jnp.bfloat16).reshape(rows, TILE_COLS),
                    preferred_element_type=jnp.float32,
                )
                stacked[half, sub] = projected.astype(jnp.bfloat16)
                for step in range(1, chips):
                    gather_copy(half, step).start()
                pair_copy(half, 0).start()
        if colour + 1 < COLORS:
            for half in halves:
                correct(colour, half)

    for half in halves:
        for step in range(1, chips):
            gather_copy(half, step).wait_recv()
            pair_copy(half, step).start()
    for half in halves:
        part = lanes(half)
        for step in range(chips):
            pair_copy(half, step).wait_recv()
        coarse = jnp.dot(
            coarse_ref[...],
            stacked[half].reshape(subs * cp, TILE_COLS),
            preferred_element_type=jnp.float32,
        ).astype(jnp.bfloat16)
        lifted = lax.dot_general(
            restriction_ref[...],
            coarse,
            (((0,), (0,)), ((), ())),
            preferred_element_type=jnp.float32,
        ).reshape(block_count, BLK, TILE_COLS)
        out_ref[:, :, part] = (accumulated[:, :, part] + lifted).astype(jnp.bfloat16)

    for half in halves:
        for step in range(1, chips):
            gather_copy(half, step).wait_send()
        for step in range(chips):
            pair_copy(half, step).wait_send()
    for colour in range(COLORS):

        @on_relay
        def _():
            wait_bytes(outgoing.at[colour], pieces - 1, sem_spread_out.at[colour])
            wait_bytes(forwarded.at[colour], count - 1, sem_back_out.at[colour])

        @off_relay
        def _():
            wait_bytes(outgoing.at[colour], pieces, sem_spread_out.at[colour])


def shards(right_side, local_inverse, coupling, margin_blocks, partner, restriction, coarse_rows):
    regions, subs = lax.axis_size("region"), lax.axis_size("sub")
    count = regions * subs
    right = right_side[0, 0]
    rows, columns = right.shape
    pieces = OVL_BLK * BLK * columns // (TILE_ROWS * TILE_COLS)
    cp = restriction.shape[2]
    piece = (TILE_ROWS, TILE_COLS)
    blocked = (rows // BLK, BLK, columns)
    vmem = pl.BlockSpec(memory_space=pltpu.VMEM)
    smem = pl.BlockSpec(memory_space=pltpu.SMEM)
    hbm = pl.BlockSpec(memory_space=pltpu.HBM)
    bf16 = jnp.bfloat16
    halves = columns // TILE_COLS
    dma = pltpu.SemaphoreType.DMA
    result = pl.pallas_call(
        functools.partial(sweep, regions, subs),
        out_shape=jax.ShapeDtypeStruct(blocked, jnp.bfloat16),
        in_specs=[hbm, hbm, hbm, smem, smem, hbm, hbm],
        out_specs=vmem,
        scratch_shapes=[
            pltpu.VMEM(blocked, bf16),
            pltpu.VMEM((rows // BLK, BLK, rows), bf16),
            pltpu.VMEM(coupling.shape[2:], bf16),
            pltpu.VMEM(restriction.shape[2:], bf16),
            pltpu.VMEM(coarse_rows.shape[1:], bf16),
            dma((5,)),
            pltpu.VMEM(blocked, jnp.float32),
            pltpu.VMEM(blocked, jnp.float32),
            pltpu.VMEM((rows, columns), jnp.bfloat16),
            pltpu.VMEM((COLORS, pieces) + piece, jnp.bfloat16),
            [pltpu.VMEM((count,) + piece, jnp.bfloat16) for _ in range(COLORS)],
            pltpu.VMEM((COLORS, count) + piece, jnp.bfloat16),
            pltpu.VMEM((COLORS, pieces) + piece, jnp.bfloat16),
            pltpu.VMEM((halves, subs, cp, TILE_COLS), jnp.bfloat16),
            dma((COLORS,)),
            dma((COLORS,)),
            dma((COLORS,)),
            dma((COLORS, halves)),
            dma((halves, subs // 2)),
            dma((halves, subs // 2)),
            dma((halves, subs // 2)),
            dma((halves, subs // 2)),
        ],
        compiler_params=pltpu.CompilerParams(
            collective_id=0, has_side_effects=True, vmem_limit_bytes=56 * 1024 * 1024
        ),
    )(
        right.reshape(blocked),
        local_inverse.reshape(rows // BLK, BLK, rows),
        coupling[0, 0],
        margin_blocks[:, 0, 0, :].T,
        partner,
        restriction[0, 0],
        coarse_rows[0],
    )
    return result.reshape(right_side.shape)


def solution(mesh):
    placed = (
        P("region", "sub", None, None),
        P("region", "sub", None, None),
        P("region", "sub", None, None, None),
        P(None, "region", "sub", None),
        P(),
        P("region", "sub", None, None),
        P("region", "sub", None),
    )
    return jax.shard_map(
        shards,
        mesh=mesh,
        in_specs=placed,
        out_specs=P("region", "sub", None, None),
        check_vma=False,
    )
```

time: 69.9 us -> 64.7 us (0.926)
  local copies, waits for them, and re-layouts: 7.72 us -> 1.87 us
  Pallas kernels: 61.8 us -> 62.6 us
    unnamed x13 -> x1, local copies, waits for them, and re-layouts: 6.96 us -> 1.87 us
    pallas_call x1, Pallas kernels: 61.8 us -> 62.6 us  [shards(): pl.pallas_call(functools.partial(sweep, regions, subs), out_shape=jax.Sha...]
    squeeze x1 -> x0, local copies, waits for them, and re-layouts: 0.76 us -> none  [shards(): margin_blocks[:, 0, 0, :]]
where the time goes in v2:
time: 64.7 us; the launch traced here: 64.5 us
  Pallas kernels  62.6 us (97%)
  local copies, waits for them, and re-layouts  1.87 us (3%)
    pallas_call x1, Pallas kernels, shards(): pl.pallas_call(functools.partial(sweep, regions, subs), out_shape=jax.Sha...  62.6 us
    unnamed x1, local copies, waits for them, and re-layouts  1.87 us

profile of v2, /device:TPU:1, one launch (start us, length us, event | category | flops | bytes accessed | tf_op | source)
XLA Modules:
  0.0 64.5 jit_solution(15735052183610530696)
XLA Ops:
  0.0 62.6 %shard_map.73 = bf16[8,128,256]{2,1,0:T(8,128)(2,1)} custom-call(bf16[8,128,256]{2,1,0:T(8,128)(2,1)} %bitcast.11, bf16[8,128,1024]{2,1,0:T(8,128)(2,1)} %bitcast.10, bf16[4,256,256]{2,1,0:T(8,128)(2,1)} %bitcast.12, s32[2,4]{1,0:T(2,128)} %bitcast.15, s32[4,32]{1,0:T(4,128)} %partner_ref.1, bf16[64,1024]{1,0:T(8,128)(2,1)} %bitcast.13, ...), custom_call_target="tpu_custom_call" | custom-call | tf_op jit(solution)/shard_map/pallas_call | solution.py:328
  62.6 1.9 %copy.9 = bf16[1,1,1024,256]{3,2,1,0:T(8,128)(2,1)} copy(bf16[1,1,1024,256]{3,2,1,0:T(8,128)(2,1)} %bitcast.9) | data formatting | bytes 1048576

commit v3 on v2

--- a/solution.py
+++ b/solution.py
@@ -22,11 +22,13 @@
     right_hbm,
     inverse_hbm,
     coupling_hbm,
-    blocks_ref,
-    partner_ref,
+    blocks_hbm,
+    partner_hbm,
     restriction_hbm,
     coarse_hbm,
     out_ref,
+    blocks_ref,
+    partner_ref,
     right_ref,
     inverse_ref,
     coupling_ref,
@@ -72,7 +74,9 @@
         pltpu.make_async_copy(source, target, sem_load.at[i])
         for i, (source, target) in enumerate(
             [
+                (blocks_hbm, blocks_ref),
                 (right_hbm, right_ref),
+                (partner_hbm, partner_ref),
                 (coupling_hbm, coupling_ref),
                 (inverse_hbm, inverse_ref),
                 (restriction_hbm, restriction_ref),
@@ -219,6 +223,7 @@
 
     halves = range(col_tiles)
     loads[0].wait()
+    loads[1].wait()
     for half in halves:
         for k in range(OVL_BLK):
             spread(0, half, k, right_ref[blocks_ref[k, 0]][:, lanes(half)])
@@ -226,7 +231,7 @@
     for half in halves:
         start_spread(0, half)
     residual[...] = right_ref[...].astype(jnp.float32)
-    for load in loads[1:]:
+    for load in loads[2:]:
         load.wait()
 
     for colour in range(COLORS):
@@ -320,7 +325,6 @@
     piece = (TILE_ROWS, TILE_COLS)
     blocked = (rows // BLK, BLK, columns)
     vmem = pl.BlockSpec(memory_space=pltpu.VMEM)
-    smem = pl.BlockSpec(memory_space=pltpu.SMEM)
     hbm = pl.BlockSpec(memory_space=pltpu.HBM)
     bf16 = jnp.bfloat16
     halves = columns // TILE_COLS
@@ -328,15 +332,17 @@
     result = pl.pallas_call(
         functools.partial(sweep, regions, subs),
         out_shape=jax.ShapeDtypeStruct(blocked, jnp.bfloat16),
-        in_specs=[hbm, hbm, hbm, smem, smem, hbm, hbm],
+        in_specs=[hbm] * 7,
         out_specs=vmem,
         scratch_shapes=[
+            pltpu.SMEM((OVL_BLK, COLORS), jnp.int32),
+            pltpu.SMEM(partner.shape, jnp.int32),
             pltpu.VMEM(blocked, bf16),
             pltpu.VMEM((rows // BLK, BLK, rows), bf16),
             pltpu.VMEM(coupling.shape[2:], bf16),
             pltpu.VMEM(restriction.shape[2:], bf16),
             pltpu.VMEM(coarse_rows.shape[1:], bf16),
-            dma((5,)),
+            dma((7,)),
             pltpu.VMEM(blocked, jnp.float32),
             pltpu.VMEM(blocked, jnp.float32),
             pltpu.VMEM((rows, columns), jnp.bfloat16),

time: 64.7 us -> 63.9 us (0.988)
  Pallas kernels: 62.6 us -> 61.9 us
    pallas_call x1, Pallas kernels: 62.6 us -> 61.9 us  [shards(): pl.pallas_call(functools.partial(sweep, regions, subs), out_shape=jax.Sha...]
where the time goes in v3:
time: 63.9 us; the launch traced here: 63.8 us
  Pallas kernels  61.9 us (97%)
  local copies, waits for them, and re-layouts  1.87 us (3%)
    pallas_call x1, Pallas kernels, shards(): pl.pallas_call(functools.partial(sweep, regions, subs), out_shape=jax.Sha...  61.9 us
    unnamed x1, local copies, waits for them, and re-layouts  1.87 us

profile of v3, /device:TPU:1, one launch (start us, length us, event | category | flops | bytes accessed | tf_op | source)
XLA Modules:
  0.0 63.8 jit_solution(8860916068226051413)
XLA Ops:
  0.0 61.9 %shard_map.73 = bf16[8,128,256]{2,1,0:T(8,128)(2,1)} custom-call(bf16[8,128,256]{2,1,0:T(8,128)(2,1)} %bitcast.11, bf16[8,128,1024]{2,1,0:T(8,128)(2,1)} %bitcast.10, bf16[4,256,256]{2,1,0:T(8,128)(2,1)} %bitcast.12, s32[2,4]{1,0:T(2,128)} %bitcast.15, s32[4,32]{1,0:T(4,128)} %partner_hbm.1, bf16[64,1024]{1,0:T(8,128)(2,1)} %bitcast.13, ...), custom_call_target="tpu_custom_call" | custom-call | tf_op jit(solution)/shard_map/pallas_call | solution.py:332
  61.9 1.9 %copy.9 = bf16[1,1,1024,256]{3,2,1,0:T(8,128)(2,1)} copy(bf16[1,1,1024,256]{3,2,1,0:T(8,128)(2,1)} %bitcast.9) | data formatting | bytes 1048576
